TPU v7x, 32 devices: a whole 2x2x4 slice. The times are simulated.
32 devices in a mesh: groups: 2 (over x), row: 16 (over z, y, core).
Axes of the slice: x: 2, y: 2, z: 4, core: 2. Of those that a mesh axis runs over, the one named last changes fastest.
Arguments:
- matrix_a: float32 [6144, 1024], P(('groups', 'row')), parts along dimension 0, may hold values from -2.16506351 to 2.16506351, as said below
- matrix_b: float32 [6144, 1024], P(('groups', 'row')), parts along dimension 0, may hold values from -6 to 6
Outputs:
- first_factor: float32 [2048, 1024], P(('groups', 'row')), parts along dimension 0
- factor: float32 [2048, 1024], P(('groups', 'row')), parts along dimension 0
- projection: float32 [2048, 1024], P(('groups', 'row')), parts along dimension 0
There are 2 independent parts, one for each index of `groups`. A program takes and returns all parts, laid end to end along the dimension named above; each array names one. Nothing has to cross between parts.
Inputs may be any that keep to these rules, and one draw needn't show every extreme that they name: `matrix_a`: A real matrix of full column rank.
All inputs are finite; a program needn't handle non-finite values.
Results may differ from a plain program's by a relative error of at most 0.0003.
Values sent between devices are 32-bit elements; how exact they have to be, the bound alone decides.
A program may use at most 128 MiB of HBM per device.

v0:
```python
import math

import jax
import jax.numpy as jnp
from jax import lax
from jax.sharding import PartitionSpec as P


def blocked_cholesky(gram):
    width = gram.shape[0]
    block = math.gcd(width, 256)
    highest = lax.Precision.HIGHEST
    lower = jnp.zeros_like(gram)
    for begin in range(0, width, block):
        finish = begin + block
        column = gram[begin:, begin:finish]
        if begin > 0:
            done = lower[begin:, :begin]
            column = column - jnp.dot(
                done,
                lower[begin:finish, :begin].T,
                precision=highest,
                preferred_element_type=jnp.float32,
            )
        diag_block = jnp.linalg.cholesky(column[:block])
        lower = lower.at[begin:finish, begin:finish].set(diag_block)
        if finish < width:
            below = lax.linalg.triangular_solve(
                diag_block, column[block:], left_side=False, lower=True, transpose_a=True
            )
            lower = lower.at[finish:, begin:finish].set(below)
    return lower


def local_gram(basis):
    return jnp.dot(
        basis.T, basis, precision=lax.Precision.HIGHEST, preferred_element_type=jnp.float32
    )


def first_sum(basis):
    return lax.psum(local_gram(basis), "row")


def second_sum(basis):
    return lax.psum(local_gram(basis), "row")


def apply_factor(lower, basis):
    return lax.linalg.triangular_solve(lower, basis, left_side=False, lower=True, transpose_a=True)


def per_device(matrix_a, matrix_b):
    width = matrix_a.shape[1]
    out_rows = width // lax.axis_size("row")
    start = lax.axis_index("row") * out_rows
    gram1 = first_sum(matrix_a)
    shift = jnp.trace(gram1) / (4.0 * width)
    lower1 = blocked_cholesky(gram1 + shift * jnp.eye(width, dtype=jnp.float32))
    basis1 = apply_factor(lower1, matrix_a)
    gram2 = second_sum(basis1)
    lower2 = blocked_cholesky(gram2)
    basis = apply_factor(lower2, basis1)
    upper1 = lower1.T
    first_rows = lax.dynamic_slice_in_dim(upper1, start, out_rows, 0)
    second_rows = lax.dynamic_slice_in_dim(lower2.T, start, out_rows, 0)
    factor_rows = jnp.dot(
        second_rows, upper1, precision=lax.Precision.HIGHEST, preferred_element_type=jnp.float32
    )
    projection = lax.psum_scatter(
        jnp.dot(
            basis.T, matrix_b, precision=lax.Precision.HIGHEST, preferred_element_type=jnp.float32
        ),
        "row",
        scatter_dimension=0,
        tiled=True,
    )
    return (first_rows, factor_rows, projection)


def solution(mesh):
    placed = (P(("groups", "row"), None), P(("groups", "row"), None))
    return jax.shard_map(
        per_device,
        mesh=mesh,
        in_specs=placed,
        out_specs=(
            P(("groups", "row"), None),
            P(("groups", "row"), None),
            P(("groups", "row"), None),
        ),
        check_vma=False,
    )
```

profile of v0, /device:TPU:0, one launch (start us, length us, event | category | flops | bytes accessed | tf_op | source)
XLA Modules:
  0.0 1062.8 jit_solution(6568206933507499062)
XLA Ops:
  7.2 6.9 fusion.160
  14.8 113.6 %all-reduce.6.cloned.1.call-done = f32[1024,1024]{0,1:T(8,128)} async-done(((f32[1024,1024]{0,1:T(8,128)}), f32[1024,1024]{0,1:T(8,128)}) %all-reduce.6.cloned.1.call-update) | async-done | bytes 4194320 | tf_op jit(solution)/shard_map/psum | solution.py:42
  128.3 2.9 select_reduce_fusion
  131.9 2.6 select_add_fusion
  137.6 11.7 %cholesky.382 = f32[128,128]{1,0:T(8,128)S(1)} custom-call(f32[128,128]{1,0:T(8,128)S(1)} %cholesky.650), custom_call_target="Cholesky" | custom-call | tf_op jit(solution)/shard_map/jit(cholesky)/cholesky | solution.py:25
  149.3 9.8 custom-call.31
  159.8 11.7 %cholesky.399 = f32[128,128]{1,0:T(8,128)S(1)} custom-call(f32[128,128]{1,0:T(8,128)S(1)} %convolution_subtract_fusion.33), custom_call_target="Cholesky" | custom-call | tf_op jit(solution)/shard_map/jit(cholesky)/cholesky | solution.py:25
  173.7 4.0 while.30
  177.7 19.9 %custom-call.32 = f32[2,128,128]{1,2,0:T(8,128)S(1)} custom-call(f32[2,128,128]{2,1,0:T(8,128)S(1)} %get-tuple-element.232), custom_call_target="InvertDiagBlocksLowerTriangular" | custom-call | tf_op jit(solution)/shard_map/triangular_solve/custom-call.0 | solution.py:28
  203.8 11.7 %cholesky.416 = f32[128,128]{1,0:T(8,128)S(1)} custom-call(f32[128,128]{1,0:T(8,128)S(1)} %cholesky.653), custom_call_target="Cholesky" | custom-call | tf_op jit(solution)/shard_map/jit(cholesky)/cholesky | solution.py:25
  215.5 9.8 custom-call.33
  226.0 2.5 scatter.46
  229.5 12.1 %cholesky.433 = f32[128,128]{1,0:T(8,128)S(1)} custom-call(f32[128,128]{1,0:T(8,128)S(1)} %convolution_subtract_fusion.32), custom_call_target="Cholesky" | custom-call | tf_op jit(solution)/shard_map/jit(cholesky)/cholesky | solution.py:25
  245.0 4.0 while.31
  249.0 19.7 %custom-call.34 = f32[2,128,128]{1,2,0:T(8,128)S(1)} custom-call(f32[2,128,128]{2,1,0:T(8,128)S(1)} %get-tuple-element.233), custom_call_target="InvertDiagBlocksLowerTriangular" | custom-call | tf_op jit(solution)/shard_map/triangular_solve/custom-call.4 | solution.py:28
  271.2 2.6 convolution_subtract_fusion.3
  274.0 11.7 %cholesky.450 = f32[128,128]{1,0:T(8,128)S(1)} custom-call(f32[128,128]{1,0:T(8,128)S(1)} %cholesky.656), custom_call_target="Cholesky" | custom-call | tf_op jit(solution)/shard_map/jit(cholesky)/cholesky | solution.py:25
  285.8 9.8 custom-call.35
  296.3 11.9 %cholesky.467 = f32[128,128]{1,0:T(8,128)S(1)} custom-call(f32[128,128]{1,0:T(8,128)S(1)} %convolution_subtract_fusion.31), custom_call_target="Cholesky" | custom-call | tf_op jit(solution)/shard_map/jit(cholesky)/cholesky | solution.py:25
  311.6 4.0 while.32
  315.6 19.7 %custom-call.36 = f32[2,128,128]{1,2,0:T(8,128)S(1)} custom-call(f32[2,128,128]{2,1,0:T(8,128)S(1)} %get-tuple-element.234), custom_call_target="InvertDiagBlocksLowerTriangular" | custom-call | tf_op jit(solution)/shard_map/triangular_solve/custom-call.5 | solution.py:28
  339.6 11.7 %cholesky.484 = f32[128,128]{1,0:T(8,128)S(1)} custom-call(f32[128,128]{1,0:T(8,128)S(1)} %cholesky.659), custom_call_target="Cholesky" | custom-call | tf_op jit(solution)/shard_map/jit(cholesky)/cholesky | solution.py:25
  351.3 9.8 custom-call.37
  361.8 11.7 %cholesky.501 = f32[128,128]{1,0:T(8,128)S(1)} custom-call(f32[128,128]{1,0:T(8,128)S(1)} %convolution_subtract_fusion.30), custom_call_target="Cholesky" | custom-call | tf_op jit(solution)/shard_map/jit(cholesky)/cholesky | solution.py:25
  377.3 4.8 fusion.1
  382.1 23.2 %while.33 = (s32[]{:T(128)}, f32[1024,1024]{1,0:T(8,128)}, s32[8,2]{0,1:T(2,128)S(1)}, f32[8,128,128]{2,1,0:T(8,128)S(1)}, s32[]{:T(128)}) while((s32[]{:T(128)}, f32[1024,1024]{1,0:T(8,128)}, s32[8,2]{0,1:T(2,128)S(1)}, f32[8,128,128]{2,1,0:T(8,128)S(1)}, s32[]{:T(128)}) %tuple.267), condition=%wide.while_cond.17, body=%wide.while_body.17.sunk | while | flops 2 | bytes 131181 | solution.py:50
  382.7 2.3 bitcast_dynamic-update-slice_fusion.19
  385.6 2.3 bitcast_dynamic-update-slice_fusion.19
  405.3 79.2 %custom-call.38 = f32[8,128,128]{1,2,0:T(8,128)} custom-call(f32[8,128,128]{2,1,0:T(8,128)S(1)} %get-tuple-element.235), custom_call_target="InvertDiagBlocksLowerTriangular" | custom-call | tf_op jit(solution)/shard_map/triangular_solve/custom-call.6 | solution.py:50
  502.6 5.1 fusion.161
  508.0 110.3 %all-reduce.8.cloned.1.call-done = f32[1024,1024]{0,1:T(8,128)} async-done(((f32[1024,1024]{0,1:T(8,128)}), f32[1024,1024]{0,1:T(8,128)}) %all-reduce.8.cloned.1.call-update) | async-done | bytes 4194320 | tf_op jit(solution)/shard_map/psum | solution.py:46
  620.3 11.7 %cholesky.518 = f32[128,128]{1,0:T(8,128)S(1)} custom-call(f32[128,128]{1,0:T(8,128)S(1)} %cholesky.662), custom_call_target="Cholesky" | custom-call | tf_op jit(solution)/shard_map/jit(cholesky)/cholesky | solution.py:25
  632.1 9.8 custom-call.39
  642.6 11.7 %cholesky.535 = f32[128,128]{1,0:T(8,128)S(1)} custom-call(f32[128,128]{1,0:T(8,128)S(1)} %convolution_subtract_fusion.29), custom_call_target="Cholesky" | custom-call | tf_op jit(solution)/shard_map/jit(cholesky)/cholesky | solution.py:25
  657.0 3.9 while.34
  660.9 20.1 %custom-call.40 = f32[2,128,128]{1,2,0:T(8,128)S(1)} custom-call(f32[2,128,128]{2,1,0:T(8,128)S(1)} %get-tuple-element.236), custom_call_target="InvertDiagBlocksLowerTriangular" | custom-call | tf_op jit(solution)/shard_map/triangular_solve/custom-call.0 | solution.py:28
  687.2 11.7 %cholesky.552 = f32[128,128]{1,0:T(8,128)S(1)} custom-call(f32[128,128]{1,0:T(8,128)S(1)} %cholesky.665), custom_call_target="Cholesky" | custom-call | tf_op jit(solution)/shard_map/jit(cholesky)/cholesky | solution.py:25
  698.9 9.8 custom-call.41
  709.4 2.5 scatter.59
  712.9 11.9 %cholesky.569 = f32[128,128]{1,0:T(8,128)S(1)} custom-call(f32[128,128]{1,0:T(8,128)S(1)} %convolution_subtract_fusion.28), custom_call_target="Cholesky" | custom-call | tf_op jit(solution)/shard_map/jit(cholesky)/cholesky | solution.py:25
  728.1 3.7 while.35
  731.8 19.7 %custom-call.42 = f32[2,128,128]{1,2,0:T(8,128)S(1)} custom-call(f32[2,128,128]{2,1,0:T(8,128)S(1)} %get-tuple-element.237), custom_call_target="InvertDiagBlocksLowerTriangular" | custom-call | tf_op jit(solution)/shard_map/triangular_solve/custom-call.4 | solution.py:28
  753.9 2.6 convolution_subtract_fusion.2
  756.7 11.7 %cholesky.586 = f32[128,128]{1,0:T(8,128)S(1)} custom-call(f32[128,128]{1,0:T(8,128)S(1)} %cholesky.668), custom_call_target="Cholesky" | custom-call | tf_op jit(solution)/shard_map/jit(cholesky)/cholesky | solution.py:25
  768.5 9.8 custom-call.43
  779.0 12.1 %cholesky.603 = f32[128,128]{1,0:T(8,128)S(1)} custom-call(f32[128,128]{1,0:T(8,128)S(1)} %convolution_subtract_fusion.27), custom_call_target="Cholesky" | custom-call | tf_op jit(solution)/shard_map/jit(cholesky)/cholesky | solution.py:25
  794.4 3.8 while.36
  798.2 19.7 %custom-call.44 = f32[2,128,128]{1,2,0:T(8,128)S(1)} custom-call(f32[2,128,128]{2,1,0:T(8,128)S(1)} %get-tuple-element.238), custom_call_target="InvertDiagBlocksLowerTriangular" | custom-call | tf_op jit(solution)/shard_map/triangular_solve/custom-call.5 | solution.py:28
  822.2 11.7 %cholesky.620 = f32[128,128]{1,0:T(8,128)S(1)} custom-call(f32[128,128]{1,0:T(8,128)S(1)} %cholesky.671), custom_call_target="Cholesky" | custom-call | tf_op jit(solution)/shard_map/jit(cholesky)/cholesky | solution.py:25
  833.9 9.8 custom-call.45
  844.4 11.7 %cholesky.637 = f32[128,128]{1,0:T(8,128)S(1)} custom-call(f32[128,128]{1,0:T(8,128)S(1)} %convolution_subtract_fusion.26), custom_call_target="Cholesky" | custom-call | tf_op jit(solution)/shard_map/jit(cholesky)/cholesky | solution.py:25
  859.7 4.7 fusion
  864.4 23.9 %while.37 = (s32[]{:T(128)}, f32[1024,1024]{1,0:T(8,128)}, s32[8,2]{0,1:T(2,128)S(1)}, f32[8,128,128]{2,1,0:T(8,128)S(1)}, s32[]{:T(128)}) while((s32[]{:T(128)}, f32[1024,1024]{1,0:T(8,128)}, s32[8,2]{0,1:T(2,128)S(1)}, f32[8,128,128]{2,1,0:T(8,128)S(1)}, s32[]{:T(128)}) %tuple.288), condition=%wide.while_cond.17.clone, body=%wide.while_body.17.clone.sunk | while | flops 2 | bytes 131181 | solution.py:50
  865.1 2.3 bitcast_dynamic-update-slice_fusion.23
  868.1 2.3 bitcast_dynamic-update-slice_fusion.23
  871.1 2.3 bitcast_dynamic-update-slice_fusion.23
  874.1 2.3 bitcast_dynamic-update-slice_fusion.23
  877.1 2.3 bitcast_dynamic-update-slice_fusion.23
  880.1 2.3 bitcast_dynamic-update-slice_fusion.23
  883.1 2.3 bitcast_dynamic-update-slice_fusion.23
  888.3 78.6 %custom-call.46 = f32[8,128,128]{1,2,0:T(8,128)S(1)} custom-call(f32[8,128,128]{2,1,0:T(8,128)S(1)} %get-tuple-element.239), custom_call_target="InvertDiagBlocksLowerTriangular" | custom-call | tf_op jit(solution)/shard_map/triangular_solve/custom-call.6 | solution.py:50
  979.1 5.4 fusion.162
  986.7 7.4 fusion.10
  994.1 62.0 %reduce-scatter.2.cloned.1.call-done = f32[64,1024]{1,0:T(8,128)} async-done(((f32[1024,1024]{1,0:T(8,128)}), f32[64,1024]{1,0:T(8,128)}) %reduce-scatter.2.cloned.1.call-update) | async-done | bytes 262160 | tf_op jit(solution)/shard_map/reduce_scatter | solution.py:70
  (284 shorter events, 135.8 us)
Async XLA Ops:
  7.2 971.9 %copy-start = (f32[192,1024]{1,0:T(8,128)S(1)}, f32[192,1024]{1,0:T(8,128)}, u32[]{:S(2)}) copy-start(f32[192,1024]{1,0:T(8,128)} %param.40) | copy-start | bytes 2359300
  7.2 121.1 %all-reduce.6.cloned.1.call-start = ((), (), s32[]{:S(2)}) async-start(), calls=%async_computation.1 | async-start | bytes 8388608 | tf_op jit(solution)/shard_map/psum | solution.py:42
  14.2 604.1 %all-reduce.8.cloned.1.call-start = ((), (), s32[]{:S(2)}) async-start(), calls=%async_computation.2 | async-start | bytes 8388608 | tf_op jit(solution)/shard_map/psum | solution.py:46
  134.5 1.9 copy-start.1
  377.3 107.2 %copy-start.2 = (f32[192,1024]{1,0:T(8,128)S(1)}, f32[192,1024]{1,0:T(8,128)}, u32[]{:S(2)}) copy-start(f32[192,1024]{1,0:T(8,128)} %param.39) | copy-start | bytes 2359300
  484.6 9.6 copy-start.3
  507.7 548.3 %reduce-scatter.2.cloned.1.call-start = ((), (), s32[]{:S(2)}) async-start(), calls=%async_computation.3 | async-start | bytes 4456448 | tf_op jit(solution)/shard_map/reduce_scatter | solution.py:70
  864.4 107.3 %copy-start.5 = (f32[192,128]{1,0:T(8,128)S(1)}, f32[192,128]{1,0:T(8,128)}, u32[]{:S(2)}) copy-start(f32[192,128]{1,0:T(8,128)} %get-tuple-element.421) | copy-start | bytes 294916
  864.4 109.0 %copy-start.7 = (f32[192,128]{1,0:T(8,128)S(1)}, f32[192,128]{1,0:T(8,128)}, u32[]{:S(2)}) copy-start(f32[192,128]{1,0:T(8,128)} %get-tuple-element.422) | copy-start | bytes 294916
  864.4 110.8 %copy-start.4 = (f32[192,128]{1,0:T(8,128)S(1)}, f32[192,128]{1,0:T(8,128)}, u32[]{:S(2)}) copy-start(f32[192,128]{1,0:T(8,128)} %get-tuple-element.423) | copy-start | bytes 294916
  966.9 10.1 copy-start.6
Sparse Core Ops, SparseCore 0:
  14.3 113.9 all-reduce.5
  507.9 110.3 all-reduce.7
  984.7 71.3 reduce-scatter.1
where the time goes:
time: 1070 us; the launch traced here: 1060 us
  other arithmetic  581 us (54%)
  waiting for transfers between devices  286 us (27%)
  matrix products  85.5 us (8%)
  local copies, waits for them, and re-layouts  83 us (8%)
  between operations  26.5 us (2%)
    another operation x55, other arithmetic, blocked_cholesky(): diag_block = jnp.linalg.cholesky(column[:block])  277 us
    another operation x5, other arithmetic, apply_factor(): lax.linalg.triangular_solve(lower, basis, left_side=False, lower=True, tr...  167 us
    another operation x13, other arithmetic, blocked_cholesky(): lax.linalg.triangular_solve(diag_block, column[block:], left_side=False,...  122 us
    psum x1, waiting for transfers between devices, first_sum(): return lax.psum(local_gram(basis), 'row')  114 us
    psum x1, waiting for transfers between devices, second_sum(): return lax.psum(local_gram(basis), 'row')  110 us
    reduce_scatter x1, waiting for transfers between devices, per_device(): lax.psum_scatter(jnp.dot(basis.T, matrix_b, precision=lax.Precision.HIGHE...  62 us
    another operation x51, local copies, waits for them, and re-layouts, apply_factor(): lax.linalg.triangular_solve(lower, basis, left_side=False, lower=True, tr...  46.9 us
    another operation x30, matrix products, apply_factor(): lax.linalg.triangular_solve(lower, basis, left_side=False, lower=True, tr...  30 us
  transfers between devices with their start and end apart: 3, of which 3 were waited for; matrix products, arithmetic and copies ran while one was open for 1% of the time, Pallas kernels for 0%

commit v1 on v0

v1 whole, which is shorter than its diff:
```python
import functools
import math

import jax
import jax.numpy as jnp
from jax import lax
from jax.experimental import pallas as pl
from jax.experimental.pallas import tpu as pltpu
from jax.sharding import PartitionSpec as P

HIGHEST = lax.Precision.HIGHEST
PANEL = 8


def mm(x, y, dims):
    return lax.dot_general(
        x, y, (dims, ((), ())), precision=HIGHEST, preferred_element_type=jnp.float32
    )


def spread(row, shape):
    return jnp.broadcast_to(row, shape)


def factor_block(rows, size):
    shape = (PANEL, size)
    lane = lax.broadcasted_iota(jnp.int32, shape, 1)
    sub = lax.broadcasted_iota(jnp.int32, shape, 0)
    rows = list(rows)
    upper, lower = [], []
    for p in range(size // PANEL):
        first = p * PANEL
        inside = (lane >= first) & (lane < first + PANEL)
        right = lane >= first + PANEL
        panel = rows[p]
        cols = [spread(panel[:, first + c : first + c + 1], shape) for c in range(PANEL)]
        panel = jnp.where(inside, jnp.where(lane - first == sub, 1.0, 0.0), panel)
        pivots = jnp.ones(shape, jnp.float32)
        inverse = jnp.ones(shape, jnp.float32)
        for t in range(PANEL):
            pivot = spread(cols[t][t : t + 1, :], shape)
            one_over = 1.0 / pivot
            pivots = jnp.where(sub == t, pivot, pivots)
            inverse = jnp.where(sub == t, one_over, inverse)
            if t + 1 < PANEL:
                mult = jnp.where(sub > t, cols[t] * one_over, 0.0)
                for c in range(t + 1, PANEL):
                    cols[c] = cols[c] - mult * spread(cols[c][t : t + 1, :], shape)
                panel = panel - mult * spread(panel[t : t + 1, :], shape)
        if first + PANEL < size:
            weights = jnp.where(right, panel * inverse, 0.0)
            update = mm(weights, panel, ((0,), (0,)))
            for q in range(p + 1, size // PANEL):
                kept = jnp.where(inside, 0.0, rows[q])
                rows[q] = kept - update[q * PANEL : (q + 1) * PANEL]
        scale = 1.0 / jnp.sqrt(pivots)
        corner = jnp.zeros(shape, jnp.float32)
        for c in range(PANEL):
            corner = jnp.where((lane == first + c) & (sub <= c), cols[c], corner)
        upper.append(jnp.where(right, panel, corner) * scale)
        lower.append(jnp.where(right, 0.0, panel) * scale)
    return jnp.concatenate(upper, axis=0), jnp.concatenate(lower, axis=0)


def factor_kernel(block, g_ref, r_ref, t_ref, pan):
    width = g_ref.shape[0]
    blocks = width // block
    t_ref[...] = g_ref[...]
    column = lax.broadcasted_iota(jnp.int32, (block, width), 1)

    def step(k, carry):
        begin = pl.multiple_of(k * block, block)
        own = pl.ds(begin, block)
        rows = [
            t_ref[pl.ds(pl.multiple_of(begin + p * PANEL, PANEL), PANEL), own]
            for p in range(block // PANEL)
        ]
        upper, lower = factor_block(rows, block)
        pan[...] = mm(lower, t_ref[own, :], ((1,), (0,)))
        pan[:, own] = lower

        def trail(i, inner):
            other = pl.ds(pl.multiple_of(i * block, block), block)
            t_ref[other, own] = jnp.zeros((block, block), jnp.float32)
            t_ref[other, :] = t_ref[other, :] - mm(pan[:, other], pan[...], ((0,), (0,)))
            return inner

        lax.fori_loop(k + 1, blocks, trail, 0)
        after = column >= begin + block
        r_ref[own, :] = jnp.where(after, pan[...], 0.0)
        r_ref[own, own] = upper
        t_ref[own, :] = jnp.where(after, 0.0, pan[...])
        return carry

    lax.fori_loop(0, blocks, step, 0)


def factor_pair(gram):
    width = gram.shape[0]
    block = math.gcd(width, 128)
    whole = jax.ShapeDtypeStruct((width, width), jnp.float32)
    return pl.pallas_call(
        functools.partial(factor_kernel, block),
        out_shape=(whole, whole),
        in_specs=[pl.BlockSpec(memory_space=pltpu.VMEM)],
        out_specs=(pl.BlockSpec(memory_space=pltpu.VMEM),) * 2,
        scratch_shapes=[pltpu.VMEM((block, width), jnp.float32)],
        compiler_params=pltpu.CompilerParams(vmem_limit_bytes=40 * 1024 * 1024),
        cost_estimate=pl.CostEstimate(
            flops=100 * width**3, bytes_accessed=12 * width * width, transcendentals=0
        ),
    )(gram)


def per_device(matrix_a, matrix_b):
    width = matrix_a.shape[1]
    out_rows = width // lax.axis_size("row")
    start = lax.axis_index("row") * out_rows
    gram1 = lax.psum(mm(matrix_a, matrix_a, ((0,), (0,))), "row")
    cross = mm(matrix_a, matrix_b, ((0,), (0,)))
    gram1, cross = lax.optimization_barrier((gram1, cross))
    cross = lax.psum(cross, "row")
    shift = jnp.trace(gram1) / (4.0 * width)
    upper1, inverse1 = factor_pair(gram1 + shift * jnp.eye(width, dtype=jnp.float32))
    inverse1, cross = lax.optimization_barrier((inverse1, cross))
    basis1 = mm(matrix_a, inverse1, ((1,), (1,)))
    gram2 = lax.psum(mm(basis1, basis1, ((0,), (0,))), "row")
    partial = mm(inverse1, cross, ((1,), (0,)))
    upper2, inverse2 = factor_pair(gram2)
    first_rows = lax.dynamic_slice_in_dim(upper1, start, out_rows, 0)
    second_rows = lax.dynamic_slice_in_dim(upper2, start, out_rows, 0)
    inverse_rows = lax.dynamic_slice_in_dim(inverse2, start, out_rows, 0)
    factor_rows = mm(second_rows, upper1, ((1,), (0,)))
    projection = mm(inverse_rows, partial, ((1,), (0,)))
    return (first_rows, factor_rows, projection)


def solution(mesh):
    placed = P(("groups", "row"), None)
    return jax.shard_map(
        per_device,
        mesh=mesh,
        in_specs=(placed, placed),
        out_specs=(placed, placed, placed),
        check_vma=False,
    )
```

time: 1070 us -> 466 us (0.44)
  other arithmetic: 581 us -> 7.72 us
  Pallas kernels: 0 us -> 165 us
  local copies, waits for them, and re-layouts: 83 us -> 11 us
  waiting for transfers between devices: 286 us -> 223 us
  matrix products: 85.5 us -> 45 us
  between operations: 26.5 us -> 14.5 us
    another operation x73 -> x0, other arithmetic: 566 us -> none  [the longest x55 277 us: blocked_cholesky(): diag_block = jnp.linalg.cholesky(column[:block])]
    pallas_call x0 -> x2, Pallas kernels: none -> 165 us  [factor_pair(): pl.pallas_call(functools.partial(factor_kernel, block), out_shape=(whole,...]
    another operation x132 -> x0, local copies, waits for them, and re-layouts: 71.8 us -> none  [the longest x51 46.9 us: apply_factor(): lax.linalg.triangular_solve(lower, basis, left_side=False, lower=True, tr...]
    reduce_scatter x1 -> x0, waiting for transfers between devices: 62 us -> none  [per_device(): lax.psum_scatter(jnp.dot(basis.T, matrix_b, precision=lax.Precision.HIGHE...]
    another operation x64 -> x0, matrix products: 46.9 us -> none  [the longest x30 30 us: apply_factor(): lax.linalg.triangular_solve(lower, basis, left_side=False, lower=True, tr...]
    dot_general x10 -> x7, matrix products: 38.5 us -> 45 us  [mm(): lax.dot_general(x, y, (dims, ((), ())), precision=HIGHEST, preferred_elem...]
    psum x2 -> x3, waiting for transfers between devices: 224 us -> 223 us  [the longest x1 109 us: per_device(): gram1 = lax.psum(mm(matrix_a, matrix_a, ((0,), (0,))), 'row')]
  transfers between devices with their start and end apart: 3 -> 3, of which waited for: 3 -> 3; matrix products, arithmetic and copies ran while one was open for 1% -> 5% of each run, Pallas kernels for 0% -> 18%
where the time goes in v1:
time: 466 us
  waiting for transfers between devices  223 us (48%)
  Pallas kernels  165 us (35%)
  matrix products  45 us (10%)
  between operations  14.5 us (3%)
  local copies, waits for them, and re-layouts  11 us (2%)
  other arithmetic  7.72 us (2%)
    pallas_call x2, Pallas kernels, factor_pair(): pl.pallas_call(functools.partial(factor_kernel, block), out_shape=(whole,...  165 us
    psum x1, waiting for transfers between devices, per_device(): gram1 = lax.psum(mm(matrix_a, matrix_a, ((0,), (0,))), 'row')  109 us
    psum x1, waiting for transfers between devices, per_device(): gram2 = lax.psum(mm(basis1, basis1, ((0,), (0,))), 'row')  91.7 us
    dot_general x7, matrix products, mm(): lax.dot_general(x, y, (dims, ((), ())), precision=HIGHEST, preferred_elem...  45 us
    psum x1, waiting for transfers between devices, per_device(): cross = lax.psum(cross, 'row')  22.3 us
    unnamed x16, local copies, waits for them, and re-layouts  9.33 us
  transfers between devices with their start and end apart: 3, of which 3 were waited for; matrix products, arithmetic and copies ran while one was open for 5% of the time, Pallas kernels for 18%

profile of v1, /device:TPU:0, one launch (start us, length us, event | category | flops | bytes accessed | tf_op | source)
XLA Modules:
  0.0 466.0 jit_solution(5355163622542590605)
XLA Ops:
  7.2 0.0 copy-start
  7.2 0.0 copy-start.7
  7.2 0.0 all-reduce.4.cloned.1.call-start
  7.2 1.1 copy-done
  8.3 5.2 %fusion.6 = f32[1024,1024]{1,0:T(8,128)} fusion(f32[192,1024]{1,0:T(8,128)S(1)} %copy-done), kind=kOutput, calls=%fused_computation.10 | convolution fusion | flops 2415919104 | bytes 4980736 | tf_op jit(solution)/shard_map/dot_general | solution.py:16
  13.5 0.0 all-reduce.4.cloned.1.call-update
  13.5 0.0 all-reduce.6.cloned.1.call-start
  13.6 0.0 copy-done.7
  13.6 5.2 %fusion.7 = f32[1024,1024]{1,0:T(8,128)} fusion(f32[192,1024]{1,0:T(8,128)S(1)} %copy-done, f32[192,1024]{1,0:T(8,128)S(1)} %copy-done.7), kind=kOutput, calls=%fused_computation.11 | convolution fusion | flops 2415919104 | bytes 5767168 | tf_op jit(solution)/shard_map/dot_general | solution.py:16
  18.8 109.1 %all-reduce.4.cloned.1.call-done = f32[1024,1024]{1,0:T(8,128)} async-done(((f32[1024,1024]{1,0:T(8,128)}), f32[1024,1024]{1,0:T(8,128)}) %all-reduce.4.cloned.1.call-update) | async-done | bytes 4194320 | tf_op jit(solution)/shard_map/psum | solution.py:119
  127.9 2.9 select_reduce_fusion
  131.4 4.8 %select_add_fusion.g_ref = f32[1024,1024]{1,0:T(8,128)} fusion(f32[1024,1024]{1,0:T(8,128)} %all-reduce.4.cloned.1.call-done, f32[]{:T(128)S(6)} %div.3), kind=kLoop, calls=%fused_computation | loop fusion | flops 3145728 | bytes 8388612 | tf_op jit(solution)/shard_map/add | solution.py:124
  136.2 0.0 all-reduce.6.cloned.1.call-update
  136.3 0.2 all-reduce.8.cloned.1.call-start
  136.5 0.0 copy-start.4
  136.5 2.2 copy-done.4
  138.7 82.1 %shard_map.49 = (f32[1024,1024]{1,0:T(8,128)S(1)}, f32[1024,1024]{1,0:T(8,128)S(1)}) custom-call(f32[1024,1024]{1,0:T(8,128)S(1)} %copy-done.4), custom_call_target="tpu_custom_call" | custom-call | flops 107374182400 | bytes 12582912 | tf_op jit(solution)/shard_map/pallas_call | solution.py:102
  220.8 0.0 copy-start.1
  220.8 1.9 copy-done.1
  222.8 0.0 copy-start.3
  222.8 1.9 copy-done.3
  224.7 22.3 %all-reduce.6.cloned.1.call-done = f32[1024,1024]{1,0:T(8,128)} async-done(((f32[1024,1024]{1,0:T(8,128)}), f32[1024,1024]{1,0:T(8,128)}) %all-reduce.6.cloned.1.call-update) | async-done | bytes 4194320 | tf_op jit(solution)/shard_map/psum | solution.py:122
  247.0 5.3 %fusion.8 = f32[1024,192]{1,0:T(8,128)S(1)} fusion(f32[1024,1024]{1,0:T(8,128)} %copy-done.3, f32[192,1024]{1,0:T(8,128)S(1)} %copy-done), kind=kOutput, calls=%fused_computation.12 | convolution fusion | flops 2415919104 | bytes 5767168 | tf_op jit(solution)/shard_map/dot_general | solution.py:16
  252.2 5.1 %fusion.9 = f32[1024,1024]{1,0:T(8,128)} fusion(f32[1024,192]{1,0:T(8,128)S(1)} %fusion.8), kind=kOutput, calls=%fused_computation.13 | convolution fusion | flops 2415919104 | bytes 4980736 | tf_op jit(solution)/shard_map/dot_general | solution.py:16
  257.3 0.0 all-reduce.8.cloned.1.call-update
  257.3 1.7 constant_dynamic-slice_fusion
  259.0 17.5 %fusion.10 = f32[1024,1024]{1,0:T(8,128)} fusion(f32[1024,1024]{1,0:T(8,128)} %copy-done.3, f32[1024,1024]{1,0:T(8,128)} %all-reduce.6.cloned.1.call-done), kind=kOutput, calls=%fused_computation.14 | convolution fusion | flops 12884901888 | bytes 12582912 | tf_op jit(solution)/shard_map/dot_general | solution.py:16
  276.5 91.7 %all-reduce.8.cloned.1.call-done.g_ref = f32[1024,1024]{1,0:T(8,128)} async-done(((f32[1024,1024]{1,0:T(8,128)}), f32[1024,1024]{1,0:T(8,128)}) %all-reduce.8.cloned.1.call-update) | async-done | bytes 4194320 | tf_op jit(solution)/shard_map/psum | solution.py:127
  368.2 0.0 copy-start.5
  368.2 2.2 copy-done.5
  370.4 0.0 copy-start.2
  370.4 82.4 %shard_map.50 = (f32[1024,1024]{1,0:T(8,128)S(1)}, f32[1024,1024]{1,0:T(8,128)S(1)}) custom-call(f32[1024,1024]{1,0:T(8,128)S(1)} %copy-done.5), custom_call_target="tpu_custom_call" | custom-call | flops 107374182400 | bytes 12582912 | tf_op jit(solution)/shard_map/pallas_call | solution.py:102
  452.8 0.0 copy-start.6
  452.8 0.0 copy-done.2
  452.8 3.4 fusion.2
  456.2 0.0 copy-done.6
  456.2 3.4 fusion
Async XLA Ops:
  7.2 1.1 copy-start
  7.2 6.4 %copy-start.7 = (f32[192,1024]{1,0:T(8,128)S(1)}, f32[192,1024]{1,0:T(8,128)}, u32[]{:S(2)}) copy-start(f32[192,1024]{1,0:T(8,128)} %param.3) | copy-start | bytes 2359300
  7.2 120.7 %all-reduce.4.cloned.1.call-start = ((), (), s32[]{:S(2)}) async-start(), calls=%async_computation | async-start | bytes 8388608 | tf_op jit(solution)/shard_map/psum | solution.py:119
  13.5 233.4 %all-reduce.6.cloned.1.call-start = ((), (), s32[]{:S(2)}) async-start(), calls=%async_computation.1 | async-start | bytes 8388608 | tf_op jit(solution)/shard_map/psum | solution.py:122
  136.3 231.9 %all-reduce.8.cloned.1.call-start = ((), (), s32[]{:S(2)}) async-start(), calls=%async_computation.2 | async-start | bytes 8388608 | tf_op jit(solution)/shard_map/psum | solution.py:127
  136.5 2.2 copy-start.4
  220.8 1.9 copy-start.1
  222.8 1.9 copy-start.3
  368.2 2.2 copy-start.5
  370.4 82.4 %copy-start.2 = (f32[1024,1024]{1,0:T(8,128)S(1)}, f32[1024,1024]{1,0:T(8,128)}, u32[]{:S(2)}) copy-start(f32[1024,1024]{1,0:T(8,128)} %copy-done.1) | copy-start | bytes 12582916
  452.8 3.4 copy-start.6
Sparse Core Ops, SparseCore 0:
  13.7 114.1 all-reduce.3
  136.4 110.5 all-reduce.5
  257.4 110.7 all-reduce.7

commit v2 on v1

--- a/solution.py
+++ b/solution.py
@@ -112,26 +112,163 @@
     )(gram)
 
 
+def sum_kernel(orders, x_ref, out_ref, *scratch):
+    lanes, steps = len(orders), len(orders[0])
+    slots = [scratch[lane * steps : (lane + 1) * steps] for lane in range(lanes)]
+    down_send, down_recv, up_send, up_recv = scratch[lanes * steps :]
+    me = lax.axis_index("row")
+    share = x_ref.shape[0] // lanes
+    bits = [lax.rem(me // (1 << b), 2) for b in range(steps)]
+    partners = [me + (1 - 2 * bits[b]) * (1 << b) for b in range(steps)]
+
+    barrier = pltpu.get_barrier_semaphore()
+    for partner in partners:
+        pl.semaphore_signal(
+            barrier, inc=1, device_id={"row": partner}, device_id_type=pl.DeviceIdType.MESH
+        )
+    pl.semaphore_wait(barrier, steps)
+
+    def source(lane, step):
+        return x_ref.at[pl.ds(lane * share, share)] if step == 0 else slots[lane][step - 1]
+
+    def halve(lane, step):
+        bit = orders[lane][step]
+        size = share >> (step + 1)
+        copy = pltpu.make_async_remote_copy(
+            src_ref=source(lane, step).at[pl.ds((1 - bits[bit]) * size, size)],
+            dst_ref=slots[lane][step],
+            send_sem=down_send.at[lane, step],
+            recv_sem=down_recv.at[lane, step],
+            device_id={"row": partners[bit]},
+            device_id_type=pl.DeviceIdType.MESH,
+        )
+        copy.start()
+        return copy
+
+    def offset(lane, level):
+        total = lane * share
+        for step in range(level):
+            total = total + bits[orders[lane][step]] * (share >> (step + 1))
+        return total
+
+    def double(lane, step):
+        bit = orders[lane][step]
+        own = pl.ds(offset(lane, step + 1), share >> (step + 1))
+        copy = pltpu.make_async_remote_copy(
+            src_ref=out_ref.at[own],
+            dst_ref=out_ref.at[own],
+            send_sem=up_send.at[lane, step],
+            recv_sem=up_recv.at[lane, step],
+            device_id={"row": partners[bit]},
+            device_id_type=pl.DeviceIdType.MESH,
+        )
+        copy.start()
+        return copy
+
+    flying = [halve(lane, 0) for lane in range(lanes)]
+    for step in range(steps):
+        for lane in range(lanes):
+            flying[lane].wait()
+            size = share >> (step + 1)
+            kept = source(lane, step)[pl.ds(bits[orders[lane][step]] * size, size)]
+            if step + 1 < steps:
+                slots[lane][step][...] = slots[lane][step][...] + kept
+                flying[lane] = halve(lane, step + 1)
+            else:
+                out_ref[pl.ds(offset(lane, steps), size)] = slots[lane][step][...] + kept
+                flying[lane] = double(lane, steps - 1)
+    for step in range(steps - 1, -1, -1):
+        for lane in range(lanes):
+            flying[lane].wait()
+            if step > 0:
+                flying[lane] = double(lane, step - 1)
+
+
+def sum_tiles(tiles, devices):
+    steps = devices.bit_length() - 1
+    straight = list(range(steps))
+    orders = (straight, straight[:1] + straight[2:] + straight[1:2])
+    share = tiles.shape[0] // len(orders)
+    slots = [
+        pltpu.VMEM((share >> (step + 1),) + tiles.shape[1:], jnp.float32)
+        for _ in orders
+        for step in range(steps)
+    ]
+    sems = [pltpu.SemaphoreType.DMA((len(orders), steps))] * 4
+    return pl.pallas_call(
+        functools.partial(sum_kernel, orders),
+        out_shape=jax.ShapeDtypeStruct(tiles.shape, jnp.float32),
+        in_specs=[pl.BlockSpec(memory_space=pltpu.VMEM)],
+        out_specs=pl.BlockSpec(memory_space=pltpu.VMEM),
+        scratch_shapes=slots + sems,
+        compiler_params=pltpu.CompilerParams(
+            collective_id=0, has_side_effects=True, vmem_limit_bytes=24 * 1024 * 1024
+        ),
+        cost_estimate=pl.CostEstimate(
+            flops=1 << 33, bytes_accessed=8 * tiles.size, transcendentals=0
+        ),
+    )(tiles)
+
+
+def to_tiles(x):
+    rows, columns = x.shape
+    return x.reshape(rows // 8, 8, columns // 128, 128).swapaxes(1, 2).reshape(-1, 8, 128)
+
+
+def from_tiles(x, columns):
+    return x.reshape(-1, columns // 128, 8, 128).swapaxes(1, 2).reshape(-1, columns)
+
+
+def sum_gram(basis):
+    devices = lax.axis_size("row")
+    width = basis.shape[1]
+    half = width // 2
+    if devices & (devices - 1) or devices < 4 or width % 256:
+        return lax.psum(mm(basis, basis, ((0,), (0,))), "row")
+    left, right = basis[:, :half], basis[:, half:]
+    top = mm(left, basis, ((0,), (0,)))
+    bottom = mm(right, right, ((0,), (0,)))
+    row = lax.broadcasted_iota(jnp.int32, (half, half), 0)
+    col = lax.broadcasted_iota(jnp.int32, (half, half), 1)
+    folded = jnp.where(row <= col, top[:, :half], bottom)
+    extra = 8
+    while (half + extra) // 8 * (width // 128) % (2 * devices):
+        extra += 8
+    ends = jnp.pad(jnp.diagonal(bottom)[None, :], ((0, extra - 1), (0, width - half)))
+    packed = jnp.concatenate([jnp.concatenate([folded, top[:, half:]], axis=1), ends], axis=0)
+    packed = from_tiles(sum_tiles(to_tiles(packed), devices), width)
+    folded, corner, ends = packed[:half, :half], packed[:half, half:], packed[half, :half]
+    turned = folded.T
+    first = jnp.where(row <= col, folded, turned)
+    second = jnp.where(row == col, ends[None, :], jnp.where(row > col, folded, turned))
+    return jnp.concatenate(
+        [
+            jnp.concatenate([first, corner], axis=1),
+            jnp.concatenate([jnp.zeros_like(corner), second], axis=1),
+        ],
+        axis=0,
+    )
+
+
 def per_device(matrix_a, matrix_b):
     width = matrix_a.shape[1]
     out_rows = width // lax.axis_size("row")
     start = lax.axis_index("row") * out_rows
-    gram1 = lax.psum(mm(matrix_a, matrix_a, ((0,), (0,))), "row")
+    gram1 = sum_gram(matrix_a)
     cross = mm(matrix_a, matrix_b, ((0,), (0,)))
     gram1, cross = lax.optimization_barrier((gram1, cross))
     cross = lax.psum(cross, "row")
     shift = jnp.trace(gram1) / (4.0 * width)
     upper1, inverse1 = factor_pair(gram1 + shift * jnp.eye(width, dtype=jnp.float32))
-    inverse1, cross = lax.optimization_barrier((inverse1, cross))
     basis1 = mm(matrix_a, inverse1, ((1,), (1,)))
-    gram2 = lax.psum(mm(basis1, basis1, ((0,), (0,))), "row")
-    partial = mm(inverse1, cross, ((1,), (0,)))
+    gram2 = sum_gram(basis1)
     upper2, inverse2 = factor_pair(gram2)
     first_rows = lax.dynamic_slice_in_dim(upper1, start, out_rows, 0)
     second_rows = lax.dynamic_slice_in_dim(upper2, start, out_rows, 0)
     inverse_rows = lax.dynamic_slice_in_dim(inverse2, start, out_rows, 0)
     factor_rows = mm(second_rows, upper1, ((1,), (0,)))
-    projection = mm(inverse_rows, partial, ((1,), (0,)))
+    inverse_rows = mm(inverse_rows, inverse1, ((1,), (0,)))
+    projection = mm(inverse_rows, cross, ((1,), (0,)))
     return (first_rows, factor_rows, projection)
 
 

time: 466 us -> 347 us (0.74)
  waiting for transfers between devices: 223 us -> 0.02 us
  Pallas kernels: 165 us -> 255 us
  local copies, waits for them, and re-layouts: 11 us -> 23.9 us
  matrix products: 45 us -> 36.7 us
  other arithmetic: 7.72 us -> 15.8 us
    psum x2 -> x0, waiting for transfers between devices: 201 us -> none  [the longest x1 109 us: per_device(): gram1 = lax.psum(mm(matrix_a, matrix_a, ((0,), (0,))), 'row')]
    pallas_call x0 -> x2, Pallas kernels: none -> 89.3 us  [sum_tiles(): pl.pallas_call(functools.partial(sum_kernel, orders), out_shape=jax.Shape...]
    psum x1, waiting for transfers between devices: 22.3 us -> 0.01 us  [per_device(): cross = lax.psum(cross, 'row')]
    gather x0 -> x2, local copies, waits for them, and re-layouts: none -> 9.28 us  [sum_gram(): jnp.diagonal(bottom)[None, :]]
    dot_general x7 -> x9, matrix products: 45 us -> 36.7 us  [mm(): lax.dot_general(x, y, (dims, ((), ())), precision=HIGHEST, preferred_elem...]
    select_n x0 -> x4, other arithmetic: none -> 6.83 us  [the longest x2 3.67 us: sum_gram(): folded = jnp.where(row <= col, top[:, :half], bottom)]
    slice x0 -> x5, local copies, waits for them, and re-layouts: none -> 4.71 us  [the longest x3 4.71 us: sum_gram(): packed[:half, :half]]
    unnamed x16 -> x18, local copies, waits for them, and re-layouts: 9.33 us -> 6.97 us
  transfers between devices with their start and end apart: 3 -> 1, of which waited for: 3 -> 0; matrix products, arithmetic and copies ran while one was open for 5% -> 11% of each run, Pallas kernels for 18% -> 61%
where the time goes in v2:
time: 347 us; the launch traced here: 346 us
  Pallas kernels  255 us (73%)
  matrix products  36.7 us (11%)
  local copies, waits for them, and re-layouts  23.9 us (7%)
  other arithmetic  15.8 us (5%)
  between operations  14.9 us (4%)
    pallas_call x2, Pallas kernels, factor_pair(): pl.pallas_call(functools.partial(factor_kernel, block), out_shape=(whole,...  165 us
    pallas_call x2, Pallas kernels, sum_tiles(): pl.pallas_call(functools.partial(sum_kernel, orders), out_shape=jax.Shape...  89.3 us
    dot_general x9, matrix products, mm(): lax.dot_general(x, y, (dims, ((), ())), precision=HIGHEST, preferred_elem...  36.7 us
    gather x2, local copies, waits for them, and re-layouts, sum_gram(): jnp.diagonal(bottom)[None, :]  9.28 us
    unnamed x18, local copies, waits for them, and re-layouts  6.97 us
  transfers between devices with their start and end apart: 1, of which 0 were waited for; matrix products, arithmetic and copies ran while one was open for 11% of the time, Pallas kernels for 61%

profile of v2, /device:TPU:0, one launch (start us, length us, event | category | flops | bytes accessed | tf_op | source)
XLA Modules:
  0.0 346.1 jit_solution(18231456708418322829)
XLA Ops:
  7.2 0.0 copy-start
  7.2 0.0 all-reduce.6.cloned.1.call-start
  7.2 2.3 fusion.6
  9.5 4.4 %fusion.8 = f32[512,1024]{1,0:T(8,128)} fusion(f32[192,1024]{1,0:T(8,128)} %param.2), kind=kOutput, calls=%fused_computation.30 | convolution fusion | flops 1207959552 | bytes 3276800 | tf_op jit(solution)/shard_map/dot_general | solution.py:16
  14.0 0.3 copy.12
  14.3 4.7 %gather_fusion = f32[512]{0:T(512)S(1)} fusion(f32[512,512]{0,1:T(8,128)S(1)} %fusion.6, s32[512]{0:T(512)S(1)} %bitcast.56), kind=kCustom, calls=%fused_computation | custom fusion | bytes 8192 | tf_op jit(solution)/shard_map/jit(diagonal)/cond/branch_0_fun/gather | solution.py:237
  19.0 1.8 slice_select_fusion.1
  20.9 0.2 select_maximum_fusion.3
  21.0 44.6 %shard_map.49 = f32[544,8,128]{2,1,0:T(8,128)S(1)} custom-call(f32[544,8,128]{2,1,0:T(8,128)S(1)} %bitcast.54), custom_call_target="tpu_custom_call" | custom-call | flops 8589934592 | bytes 4456448 | tf_op jit(solution)/shard_map/pallas_call | solution.py:198
  65.6 0.5 copy.24
  66.1 0.5 copy.23
  66.6 1.1 slice.62
  67.7 2.5 copy.19
  70.2 0.0 copy-done
  70.2 6.3 %fusion.16 = f32[1024,1024]{1,0:T(8,128)} fusion(f32[192,1024]{1,0:T(8,128)} %param.2, f32[192,1024]{1,0:T(8,128)S(1)} %copy-done), kind=kOutput, calls=%fused_computation.40 | convolution fusion | flops 2415919104 | bytes 5767168 | tf_op jit(solution)/shard_map/dot_general | solution.py:16
  76.6 1.6 bitcast_select_fusion.3
  78.2 2.4 select_maximum_fusion.1
  80.6 0.0 all-reduce.6.cloned.1.call-update
  80.6 2.9 select_reduce_fusion
  84.2 2.8 select_add_fusion.g_ref
  87.0 0.0 copy-start.7
  87.1 82.7 %shard_map.50 = (f32[1024,1024]{1,0:T(8,128)S(1)}, f32[1024,1024]{1,0:T(8,128)S(1)}) custom-call(f32[1024,1024]{1,0:T(8,128)S(1)} %select_add_fusion.g_ref), custom_call_target="tpu_custom_call" | custom-call | flops 107374182400 | bytes 12582912 | tf_op jit(solution)/shard_map/pallas_call | solution.py:102
  169.7 0.0 copy-start.2
  169.7 0.0 copy-start.3
  169.7 0.0 copy-done.7
  169.8 4.5 %fusion.17 = f32[1024,192]{0,1:T(8,128)S(1)} fusion(f32[1024,1024]{1,0:T(8,128)S(1)} %get-tuple-element.11, f32[192,1024]{1,0:T(8,128)S(1)} %copy-done.7), kind=kOutput, calls=%fused_computation.41 | convolution fusion | flops 2415919104 | bytes 5767168 | tf_op jit(solution)/shard_map/dot_general | solution.py:16
  174.3 3.2 fusion.4
  177.5 0.0 copy-done.2
  177.5 0.0 copy-done.3
  177.5 1.1 fusion.2
  178.6 0.3 copy.17
  179.0 4.5 %gather_fusion.1 = f32[512]{0:T(512)S(1)} fusion(f32[512,512]{0,1:T(8,128)S(1)} %fusion.2, s32[512]{0:T(512)S(1)} %bitcast.57), kind=kCustom, calls=%fused_computation.1 | custom fusion | bytes 8192 | tf_op jit(solution)/shard_map/jit(diagonal)/cond/branch_0_fun/gather | solution.py:237
  183.5 1.8 slice_select_fusion
  185.4 0.2 select_maximum_fusion.2
  185.6 44.7 %shard_map.51 = f32[544,8,128]{2,1,0:T(8,128)S(1)} custom-call(f32[544,8,128]{2,1,0:T(8,128)S(1)} %bitcast.55), custom_call_target="tpu_custom_call" | custom-call | flops 8589934592 | bytes 4456448 | tf_op jit(solution)/shard_map/pallas_call | solution.py:198
  230.3 1.1 slice.69
  231.4 2.6 copy.18
  234.0 1.6 bitcast_select_fusion.1
  235.5 0.4 select_maximum_fusion.g_ref
  236.0 82.7 %shard_map.52 = (f32[1024,1024]{1,0:T(8,128)S(1)}, f32[1024,1024]{1,0:T(8,128)S(1)}) custom-call(f32[1024,1024]{1,0:T(8,128)S(1)} %select_maximum_fusion.g_ref), custom_call_target="tpu_custom_call" | custom-call | flops 107374182400 | bytes 12582912 | tf_op jit(solution)/shard_map/pallas_call | solution.py:102
  318.7 0.0 copy-start.5
  318.7 1.9 copy-done.5
  320.6 0.0 copy-start.6
  320.6 2.0 copy-done.6
  322.6 0.0 copy-start.4
  322.6 1.8 constant_dynamic-slice_fusion
  324.4 4.9 %fusion.10 = f32[64,1024]{1,0:T(8,128)S(1)} fusion(f32[1024,1024]{1,0:T(8,128)} %copy-done.2, f32[1024,1024]{1,0:T(8,128)} %copy-done.6, s32[]{:T(128)S(6)} %select_n.47), kind=kOutput, calls=%fused_computation.32 | convolution fusion | flops 805306368 | bytes 4718596 | tf_op jit(solution)/shard_map/dot_general | solution.py:16
  329.4 0.0 copy-start.1
  329.4 0.0 copy-done.4
  329.4 4.4 %fusion.12 = f32[64,1024]{1,0:T(8,128)} fusion(f32[1024,1024]{1,0:T(8,128)S(1)} %copy-done.4, f32[1024,1024]{1,0:T(8,128)} %copy-done.5, s32[]{:T(128)S(6)} %select_n.47), kind=kOutput, calls=%fused_computation.34 | convolution fusion | flops 805306368 | bytes 4718596 | tf_op jit(solution)/shard_map/dot_general | solution.py:16
  333.8 0.0 all-reduce.6.cloned.1.call-done
  333.8 5.5 %fusion.18 = f32[64,1024]{1,0:T(8,128)} fusion(f32[64,1024]{1,0:T(8,128)S(1)} %fusion.10, f32[1024,1024]{1,0:T(8,128)} %all-reduce.6.cloned.1.call-done), kind=kOutput, calls=%fused_computation.42 | convolution fusion | flops 805306368 | bytes 4718592 | tf_op jit(solution)/shard_map/dot_general | solution.py:16
  339.3 0.0 copy-done.1
  (3 shorter events, 0.0 us)
Async XLA Ops:
  7.2 63.1 %copy-start = (f32[192,1024]{1,0:T(8,128)S(1)}, f32[192,1024]{1,0:T(8,128)}, u32[]{:S(2)}) copy-start(f32[192,1024]{1,0:T(8,128)} %param.3) | copy-start | bytes 2359300
  7.2 326.6 %all-reduce.6.cloned.1.call-start = ((), (), s32[]{:S(2)}) async-start(), calls=%async_computation | async-start | bytes 8388608 | tf_op jit(solution)/shard_map/psum | solution.py:260
  87.0 82.7 %copy-start.7 = (f32[192,1024]{1,0:T(8,128)S(1)}, f32[192,1024]{1,0:T(8,128)}, u32[]{:S(2)}) copy-start(f32[192,1024]{1,0:T(8,128)} %param.2) | copy-start | bytes 2359300
  169.7 7.8 %copy-start.2 = (f32[1024,1024]{1,0:T(8,128)}, f32[1024,1024]{1,0:T(8,128)S(1)}, u32[]{:S(2)}) copy-start(f32[1024,1024]{1,0:T(8,128)S(1)} %get-tuple-element.11) | copy-start | bytes 12582916
  169.7 7.8 %copy-start.3 = (f32[1024,1024]{1,0:T(8,128)}, f32[1024,1024]{1,0:T(8,128)S(1)}, u32[]{:S(2)}) copy-start(f32[1024,1024]{1,0:T(8,128)S(1)} %get-tuple-element.10) | copy-start | bytes 12582916
  318.7 1.9 copy-start.5
  320.6 2.0 copy-start.6
  322.6 6.8 %copy-start.4 = (f32[1024,1024]{1,0:T(8,128)S(1)}, f32[1024,1024]{1,0:T(8,128)}, u32[]{:S(2)}) copy-start(f32[1024,1024]{1,0:T(8,128)} %copy-done.3) | copy-start | bytes 12582916
  329.4 9.9 %copy-start.1 = (f32[192,1024]{1,0:T(8,128)S(1)}, f32[192,1024]{1,0:T(8,128)}, u32[]{:S(2)}) copy-start(f32[192,1024]{1,0:T(8,128)} %param.3) | copy-start | bytes 2359300
Sparse Core Ops, SparseCore 0:
  80.7 112.3 all-reduce.5

commit v3 on v2

--- a/solution.py
+++ b/solution.py
@@ -1,5 +1,4 @@
 import functools
-import math
 
 import jax
 import jax.numpy as jnp
@@ -10,6 +9,7 @@
 
 HIGHEST = lax.Precision.HIGHEST
 PANEL = 8
+LANES = 128
 
 
 def mm(x, y, dims):
@@ -34,6 +34,11 @@
         right = lane >= first + PANEL
         panel = rows[p]
         cols = [spread(panel[:, first + c : first + c + 1], shape) for c in range(PANEL)]
+        ahead = p + 1 < size // PANEL
+        if ahead:
+            follow = rows[p + 1]
+            under = [spread(follow[:, first + c : first + c + 1], shape) for c in range(PANEL)]
+            follow = jnp.where(inside, 0.0, follow)
         panel = jnp.where(inside, jnp.where(lane - first == sub, 1.0, 0.0), panel)
         pivots = jnp.ones(shape, jnp.float32)
         inverse = jnp.ones(shape, jnp.float32)
@@ -42,15 +47,23 @@
             one_over = 1.0 / pivot
             pivots = jnp.where(sub == t, pivot, pivots)
             inverse = jnp.where(sub == t, one_over, inverse)
-            if t + 1 < PANEL:
-                mult = jnp.where(sub > t, cols[t] * one_over, 0.0)
-                for c in range(t + 1, PANEL):
-                    cols[c] = cols[c] - mult * spread(cols[c][t : t + 1, :], shape)
-                panel = panel - mult * spread(panel[t : t + 1, :], shape)
-        if first + PANEL < size:
+            mult = jnp.where(sub > t, cols[t] * one_over, 0.0)
+            whole = spread(panel[t : t + 1, :], shape)
+            heads = [spread(cols[c][t : t + 1, :], shape) for c in range(t + 1, PANEL)]
+            for c, head in zip(range(t + 1, PANEL), heads):
+                cols[c] = cols[c] - mult * head
+            panel = panel - mult * whole
+            if ahead:
+                low = under[t] * one_over
+                for c, head in zip(range(t + 1, PANEL), heads):
+                    under[c] = under[c] - low * head
+                follow = follow - low * whole
+        if ahead:
+            rows[p + 1] = follow
+        if p + 2 < size // PANEL:
             weights = jnp.where(right, panel * inverse, 0.0)
             update = mm(weights, panel, ((0,), (0,)))
-            for q in range(p + 1, size // PANEL):
+            for q in range(p + 2, size // PANEL):
                 kept = jnp.where(inside, 0.0, rows[q])
                 rows[q] = kept - update[q * PANEL : (q + 1) * PANEL]
         scale = 1.0 / jnp.sqrt(pivots)
@@ -62,10 +75,47 @@
     return jnp.concatenate(upper, axis=0), jnp.concatenate(lower, axis=0)
 
 
-def factor_kernel(block, g_ref, r_ref, t_ref, pan):
-    width = g_ref.shape[0]
+def unfold(x_ref, t_ref, width, shifted):
+    half, parts = width // 2, width // (2 * LANES)
+    row = lax.broadcasted_iota(jnp.int32, (LANES, LANES), 0)
+    col = lax.broadcasted_iota(jnp.int32, (LANES, LANES), 1)
+    tiles = LANES // 8
+
+    def place(i, j, value):
+        t_ref[i * LANES : (i + 1) * LANES, j * LANES : (j + 1) * LANES] = value
+
+    for i in range(2 * parts):
+        for j in range(i):
+            place(i, j, jnp.zeros((LANES, LANES), jnp.float32))
+    trace = jnp.zeros((1, 1), jnp.float32)
+    for i in range(parts):
+        for j in range(2 * parts):
+            value = x_ref[i * tiles : (i + 1) * tiles, j].reshape(LANES, LANES)
+            if j >= parts or i < j:
+                place(i, j, value)
+            elif i > j:
+                place(parts + j, parts + i, value.T)
+            else:
+                turned = value.T
+                ends = x_ref[half // 8, j][0:1, :]
+                place(i, i, jnp.where(row <= col, value, turned))
+                lower = jnp.where(row > col, value, turned)
+                place(parts + i, parts + i, jnp.where(row == col, ends, lower))
+                if shifted:
+                    pivots = jnp.where(row == col, value + ends, 0.0)
+                    line = jnp.sum(pivots, axis=0, keepdims=True)
+                    trace = trace + jnp.sum(line, axis=1, keepdims=True)
+    if shifted:
+        shift = trace * (1.0 / (4.0 * width))
+        for i in range(2 * parts):
+            own = slice(i * LANES, (i + 1) * LANES)
+            t_ref[own, own] = t_ref[own, own] + jnp.where(row == col, shift, 0.0)
+
+
+def factor_kernel(block, shifted, x_ref, r_ref, t_ref, pan):
+    width = t_ref.shape[0]
     blocks = width // block
-    t_ref[...] = g_ref[...]
+    unfold(x_ref, t_ref, width, shifted)
     column = lax.broadcasted_iota(jnp.int32, (block, width), 1)
 
     def step(k, carry):
@@ -95,21 +145,63 @@
     lax.fori_loop(0, blocks, step, 0)
 
 
-def factor_pair(gram):
-    width = gram.shape[0]
-    block = math.gcd(width, 128)
+def factor_pair(folded, width, shifted):
     whole = jax.ShapeDtypeStruct((width, width), jnp.float32)
     return pl.pallas_call(
-        functools.partial(factor_kernel, block),
+        functools.partial(factor_kernel, LANES, shifted),
         out_shape=(whole, whole),
         in_specs=[pl.BlockSpec(memory_space=pltpu.VMEM)],
         out_specs=(pl.BlockSpec(memory_space=pltpu.VMEM),) * 2,
-        scratch_shapes=[pltpu.VMEM((block, width), jnp.float32)],
+        scratch_shapes=[pltpu.VMEM((LANES, width), jnp.float32)],
         compiler_params=pltpu.CompilerParams(vmem_limit_bytes=40 * 1024 * 1024),
         cost_estimate=pl.CostEstimate(
             flops=100 * width**3, bytes_accessed=12 * width * width, transcendentals=0
         ),
-    )(gram)
+    )(folded)
+
+
+def gram_kernel(basis_ref, x_ref):
+    width = basis_ref.shape[1]
+    half, parts = width // 2, width // (2 * LANES)
+    tiles = LANES // 8
+    row = lax.broadcasted_iota(jnp.int32, (LANES, LANES), 0)
+    col = lax.broadcasted_iota(jnp.int32, (LANES, LANES), 1)
+    x_ref[half // 8 :] = jnp.zeros((x_ref.shape[0] - half // 8,) + x_ref.shape[1:], jnp.float32)
+    for i in range(parts):
+        left = basis_ref[:, i * LANES : (i + 1) * LANES]
+        right = basis_ref[:, half + i * LANES : half + (i + 1) * LANES]
+        upper = mm(left, basis_ref[:, i * LANES :], ((0,), (0,)))
+        lower = mm(right, basis_ref[:, half : half + (i + 1) * LANES], ((0,), (0,)))
+        for j in range(2 * parts):
+            if j >= i:
+                above = upper[:, (j - i) * LANES : (j - i + 1) * LANES]
+            if j <= i:
+                below = lower[:, j * LANES : (j + 1) * LANES]
+            if j == i:
+                value = jnp.where(row <= col, above, below)
+                line = jnp.sum(jnp.where(row == col, below, 0.0), axis=0, keepdims=True)
+                x_ref[half // 8, j, 0:1, :] = line
+            else:
+                value = above if j > i else below
+            x_ref[i * tiles : (i + 1) * tiles, j] = value.reshape(tiles, 8, LANES)
+
+
+def folded_gram(basis, devices):
+    width = basis.shape[1]
+    lanes = width // LANES
+    count = width // 16 + 1
+    while count * lanes % (2 * devices):
+        count += 1
+    return pl.pallas_call(
+        gram_kernel,
+        out_shape=jax.ShapeDtypeStruct((count, lanes, 8, LANES), jnp.float32),
+        in_specs=[pl.BlockSpec(memory_space=pltpu.VMEM)],
+        out_specs=pl.BlockSpec(memory_space=pltpu.VMEM),
+        compiler_params=pltpu.CompilerParams(vmem_limit_bytes=24 * 1024 * 1024),
+        cost_estimate=pl.CostEstimate(
+            flops=12 * basis.shape[0] * width**2, bytes_accessed=8 * basis.size, transcendentals=0
+        ),
+    )(basis)
 
 
 def sum_kernel(orders, x_ref, out_ref, *scratch):
@@ -210,44 +302,10 @@
     )(tiles)
 
 
-def to_tiles(x):
-    rows, columns = x.shape
-    return x.reshape(rows // 8, 8, columns // 128, 128).swapaxes(1, 2).reshape(-1, 8, 128)
-
-
-def from_tiles(x, columns):
-    return x.reshape(-1, columns // 128, 8, 128).swapaxes(1, 2).reshape(-1, columns)
-
-
 def sum_gram(basis):
     devices = lax.axis_size("row")
-    width = basis.shape[1]
-    half = width // 2
-    if devices & (devices - 1) or devices < 4 or width % 256:
-        return lax.psum(mm(basis, basis, ((0,), (0,))), "row")
-    left, right = basis[:, :half], basis[:, half:]
-    top = mm(left, basis, ((0,), (0,)))
-    bottom = mm(right, right, ((0,), (0,)))
-    row = lax.broadcasted_iota(jnp.int32, (half, half), 0)
-    col = lax.broadcasted_iota(jnp.int32, (half, half), 1)
-    folded = jnp.where(row <= col, top[:, :half], bottom)
-    extra = 8
-    while (half + extra) // 8 * (width // 128) % (2 * devices):
-        extra += 8
-    ends = jnp.pad(jnp.diagonal(bottom)[None, :], ((0, extra - 1), (0, width - half)))
-    packed = jnp.concatenate([jnp.concatenate([folded, top[:, half:]], axis=1), ends], axis=0)
-    packed = from_tiles(sum_tiles(to_tiles(packed), devices), width)
-    folded, corner, ends = packed[:half, :half], packed[:half, half:], packed[half, :half]
-    turned = folded.T
-    first = jnp.where(row <= col, folded, turned)
-    second = jnp.where(row == col, ends[None, :], jnp.where(row > col, folded, turned))
-    return jnp.concatenate(
-        [
-            jnp.concatenate([first, corner], axis=1),
-            jnp.concatenate([jnp.zeros_like(corner), second], axis=1),
-        ],
-        axis=0,
-    )
+    folded = folded_gram(basis, devices)
+    return sum_tiles(folded.reshape(-1, 8, LANES), devices).reshape(folded.shape)
 
 
 def per_device(matrix_a, matrix_b):
@@ -258,11 +316,10 @@
     cross = mm(matrix_a, matrix_b, ((0,), (0,)))
     gram1, cross = lax.optimization_barrier((gram1, cross))
     cross = lax.psum(cross, "row")
-    shift = jnp.trace(gram1) / (4.0 * width)
-    upper1, inverse1 = factor_pair(gram1 + shift * jnp.eye(width, dtype=jnp.float32))
+    upper1, inverse1 = factor_pair(gram1, width, True)
     basis1 = mm(matrix_a, inverse1, ((1,), (1,)))
     gram2 = sum_gram(basis1)
-    upper2, inverse2 = factor_pair(gram2)
+    upper2, inverse2 = factor_pair(gram2, width, False)
     first_rows = lax.dynamic_slice_in_dim(upper1, start, out_rows, 0)
     second_rows = lax.dynamic_slice_in_dim(upper2, start, out_rows, 0)
     inverse_rows = lax.dynamic_slice_in_dim(inverse2, start, out_rows, 0)

time: 347 us -> 284 us (0.82)
  Pallas kernels: 255 us -> 236 us
  other arithmetic: 15.8 us -> 0 us
  local copies, waits for them, and re-layouts: 23.9 us -> 9.95 us
  matrix products: 36.7 us -> 24.5 us
    pallas_call x2 -> x4, Pallas kernels: 165 us -> 127 us  [the longest x2 122 us: factor_pair(): pl.pallas_call(functools.partial(factor_kernel, LANES, shifted), out_shap...]
    pallas_call x2, Pallas kernels: 89.3 us -> 109 us  [sum_tiles(): pl.pallas_call(functools.partial(sum_kernel, orders), out_shape=jax.Shape...]
    dot_general x9 -> x5, matrix products: 36.7 us -> 24.5 us  [mm(): lax.dot_general(x, y, (dims, ((), ())), precision=HIGHEST, preferred_elem...]
    gather x2 -> x0, local copies, waits for them, and re-layouts: 9.28 us -> none  [sum_gram(): jnp.diagonal(bottom)[None, :]]
    select_n x4 -> x0, other arithmetic: 6.83 us -> none  [the longest x2 3.67 us: sum_gram(): folded = jnp.where(row <= col, top[:, :half], bottom)]
    slice x5 -> x0, local copies, waits for them, and re-layouts: 4.71 us -> none  [the longest x3 4.71 us: sum_gram(): packed[:half, :half]]
    unnamed x18 -> x20, local copies, waits for them, and re-layouts: 6.97 us -> 8.13 us
  transfers between devices with their start and end apart: 1 -> 1, of which waited for: 0 -> 0; matrix products, arithmetic and copies ran while one was open for 11% -> 5% of each run, Pallas kernels for 61% -> 66%
where the time goes in v3:
time: 284 us
  Pallas kernels  236 us (83%)
  matrix products  24.5 us (9%)
  between operations  14.2 us (5%)
  local copies, waits for them, and re-layouts  9.95 us (4%)
    pallas_call x2, Pallas kernels, factor_pair(): pl.pallas_call(functools.partial(factor_kernel, LANES, shifted), out_shap...  122 us
    pallas_call x2, Pallas kernels, sum_tiles(): pl.pallas_call(functools.partial(sum_kernel, orders), out_shape=jax.Shape...  109 us
    dot_general x5, matrix products, mm(): lax.dot_general(x, y, (dims, ((), ())), precision=HIGHEST, preferred_elem...  24.5 us
    unnamed x20, local copies, waits for them, and re-layouts  8.13 us
  transfers between devices with their start and end apart: 1, of which 0 were waited for; matrix products, arithmetic and copies ran while one was open for 5% of the time, Pallas kernels for 66%

profile of v3, /device:TPU:0, one launch (start us, length us, event | category | flops | bytes accessed | tf_op | source)
XLA Modules:
  0.0 284.2 jit_solution(12611508026276715646)
XLA Ops:
  7.2 0.0 copy-start
  7.2 0.0 all-reduce.2.cloned.1.call-start
  7.2 0.0 copy-start.4
  7.2 1.2 copy-done.4
  8.4 2.4 shard_map.49
  10.8 0.0 copy-start.5
  10.8 44.5 %shard_map.50 = f32[544,8,128]{2,1,0:T(8,128)S(1)} custom-call(f32[544,8,128]{2,1,0:T(8,128)S(1)} %bitcast.17), custom_call_target="tpu_custom_call" | custom-call | flops 8589934592 | bytes 4456448 | tf_op jit(solution)/shard_map/pallas_call | solution.py:290
  55.4 0.0 copy-start.8
  55.4 1.4 copy-done.8
  56.8 0.0 copy-done
  56.8 0.0 copy-done.5
  56.8 5.2 %fusion.6 = f32[1024,1024]{1,0:T(8,128)} fusion(f32[192,1024]{1,0:T(8,128)S(1)} %copy-done.5, f32[192,1024]{1,0:T(8,128)S(1)} %copy-done), kind=kOutput, calls=%fused_computation.8 | convolution fusion | flops 2415919104 | bytes 5767168 | tf_op jit(solution)/shard_map/dot_general | solution.py:16
  62.0 0.0 all-reduce.2.cloned.1.call-update
  62.0 0.0 copy-start.9
  62.0 1.6 copy-done.9
  63.6 61.2 %shard_map.51 = (f32[1024,1024]{1,0:T(8,128)S(1)}, f32[1024,1024]{1,0:T(8,128)S(1)}) custom-call(f32[68,8,8,128]{3,2,1,0:T(8,128)S(1)} %bitcast.14), custom_call_target="tpu_custom_call" | custom-call | flops 107374182400 | bytes 12582912 | tf_op jit(solution)/shard_map/pallas_call | solution.py:150
  124.8 0.0 copy-start.1
  124.8 0.0 copy-start.2
  124.9 4.5 %convolution_bitcast_fusion.basis_ref = f32[192,1024]{1,0:T(8,128)S(1)} fusion(f32[1024,1024]{1,0:T(8,128)S(1)} %get-tuple-element.11, f32[192,1024]{1,0:T(8,128)S(1)} %copy-done.5), kind=kOutput, calls=%fused_computation | convolution fusion | flops 2415919104 | bytes 5767168 | tf_op jit(solution)/shard_map/dot_general | solution.py:16
  129.4 2.4 shard_map.52
  131.7 0.0 copy-done.1
  131.8 0.0 copy-done.2
  131.8 64.0 %shard_map.53 = f32[544,8,128]{2,1,0:T(8,128)S(1)} custom-call(f32[544,8,128]{2,1,0:T(8,128)S(1)} %bitcast.16), custom_call_target="tpu_custom_call" | custom-call | flops 8589934592 | bytes 4456448 | tf_op jit(solution)/shard_map/pallas_call | solution.py:290
  195.8 61.1 %shard_map.54 = (f32[1024,1024]{1,0:T(8,128)S(1)}, f32[1024,1024]{1,0:T(8,128)S(1)}) custom-call(f32[68,8,8,128]{3,2,1,0:T(8,128)S(1)} %bitcast.15), custom_call_target="tpu_custom_call" | custom-call | flops 107374182400 | bytes 12582912 | tf_op jit(solution)/shard_map/pallas_call | solution.py:150
  256.9 0.0 copy-start.6
  256.9 1.9 copy-done.6
  258.8 0.0 copy-start.7
  258.8 2.0 copy-done.7
  260.8 0.0 copy-start.3
  260.8 1.8 constant_dynamic-slice_fusion
  262.6 4.9 %fusion = f32[64,1024]{1,0:T(8,128)S(1)} fusion(f32[1024,1024]{1,0:T(8,128)} %copy-done.1, f32[1024,1024]{1,0:T(8,128)} %copy-done.7, s32[]{:T(128)S(6)} %select_n.2), kind=kOutput, calls=%fused_computation.1 | convolution fusion | flops 805306368 | bytes 4718596 | tf_op jit(solution)/shard_map/dot_general | solution.py:16
  267.5 0.0 copy-done.3
  267.5 4.3 %fusion.2 = f32[64,1024]{1,0:T(8,128)} fusion(f32[1024,1024]{1,0:T(8,128)S(1)} %copy-done.3, f32[1024,1024]{1,0:T(8,128)} %copy-done.6, s32[]{:T(128)S(6)} %select_n.2), kind=kOutput, calls=%fused_computation.3 | convolution fusion | flops 805306368 | bytes 4718596 | tf_op jit(solution)/shard_map/dot_general | solution.py:16
  271.8 0.0 all-reduce.2.cloned.1.call-done
  271.8 5.5 %fusion.7 = f32[64,1024]{1,0:T(8,128)} fusion(f32[64,1024]{1,0:T(8,128)S(1)} %fusion, f32[1024,1024]{1,0:T(8,128)} %all-reduce.2.cloned.1.call-done), kind=kOutput, calls=%fused_computation.9 | convolution fusion | flops 805306368 | bytes 4718592 | tf_op jit(solution)/shard_map/dot_general | solution.py:16
Async XLA Ops:
  7.2 49.6 %copy-start = (f32[192,1024]{1,0:T(8,128)S(1)}, f32[192,1024]{1,0:T(8,128)}, u32[]{:S(2)}) copy-start(f32[192,1024]{1,0:T(8,128)} %param.3) | copy-start | bytes 2359300
  7.2 264.7 %all-reduce.2.cloned.1.call-start = ((), (), s32[]{:S(2)}) async-start(), calls=%async_computation | async-start | bytes 8388608 | tf_op jit(solution)/shard_map/psum | solution.py:318
  7.2 1.2 copy-start.4
  10.8 46.0 %copy-start.5 = (f32[192,1024]{1,0:T(8,128)S(1)}, f32[192,1024]{1,0:T(8,128)}, u32[]{:S(2)}) copy-start(f32[192,1024]{1,0:T(8,128)} %basis_ref.1) | copy-start | bytes 2359300
  55.4 1.4 copy-start.8
  62.0 1.6 copy-start.9
  124.8 6.9 %copy-start.1 = (f32[1024,1024]{1,0:T(8,128)}, f32[1024,1024]{1,0:T(8,128)S(1)}, u32[]{:S(2)}) copy-start(f32[1024,1024]{1,0:T(8,128)S(1)} %get-tuple-element.11) | copy-start | bytes 12582916
  124.8 6.9 %copy-start.2 = (f32[1024,1024]{1,0:T(8,128)}, f32[1024,1024]{1,0:T(8,128)S(1)}, u32[]{:S(2)}) copy-start(f32[1024,1024]{1,0:T(8,128)S(1)} %get-tuple-element.10) | copy-start | bytes 12582916
  256.9 1.9 copy-start.6
  258.8 2.0 copy-start.7
  260.8 6.7 %copy-start.3 = (f32[1024,1024]{1,0:T(8,128)S(1)}, f32[1024,1024]{1,0:T(8,128)}, u32[]{:S(2)}) copy-start(f32[1024,1024]{1,0:T(8,128)} %copy-done.2) | copy-start | bytes 12582916
Sparse Core Ops, SparseCore 0:
  62.1 133.5 all-reduce.1

commit v4 on v3

--- a/solution.py
+++ b/solution.py
@@ -22,7 +22,7 @@
     return jnp.broadcast_to(row, shape)
 
 
-def factor_block(rows, size):
+def factor_block(rows, size, beside):
     shape = (PANEL, size)
     lane = lax.broadcasted_iota(jnp.int32, shape, 1)
     sub = lax.broadcasted_iota(jnp.int32, shape, 0)
@@ -40,6 +40,7 @@
             under = [spread(follow[:, first + c : first + c + 1], shape) for c in range(PANEL)]
             follow = jnp.where(inside, 0.0, follow)
         panel = jnp.where(inside, jnp.where(lane - first == sub, 1.0, 0.0), panel)
+        beside(p)
         pivots = jnp.ones(shape, jnp.float32)
         inverse = jnp.ones(shape, jnp.float32)
         for t in range(PANEL):
@@ -112,34 +113,53 @@
             t_ref[own, own] = t_ref[own, own] + jnp.where(row == col, shift, 0.0)
 
 
-def factor_kernel(block, shifted, x_ref, r_ref, t_ref, pan):
+def factor_kernel(block, shifted, x_ref, r_ref, t_ref, work, pans):
     width = t_ref.shape[0]
     blocks = width // block
-    unfold(x_ref, t_ref, width, shifted)
+    turns = block // PANEL
+    piece = width * (blocks - 1) // turns // LANES * LANES
+    while piece == 0 or width % piece or (width // piece) * (blocks - 1) > turns:
+        piece += LANES
+    pieces = width // piece
+    unfold(x_ref, work, width, shifted)
+    pans[1] = jnp.zeros(pans.shape[1:], jnp.float32)
+    pans[0, :, width:] = jnp.zeros((block, block), jnp.float32)
+    work[width:, :] = jnp.zeros((block, width), jnp.float32)
     column = lax.broadcasted_iota(jnp.int32, (block, width), 1)
+    part = lax.broadcasted_iota(jnp.int32, (block, piece), 1)
 
     def step(k, carry):
         begin = pl.multiple_of(k * block, block)
         own = pl.ds(begin, block)
+        now, before = lax.rem(k, 2), lax.rem(k + 1, 2)
+
+        def beside(p):
+            if p >= pieces * (blocks - 1):
+                return
+            target = jnp.minimum(k + 1 + p // pieces, blocks)
+            other = pl.ds(pl.multiple_of(target * block, block), block)
+            low = p % pieces * piece
+            place = slice(low, low + piece)
+            gone = (part + low >= begin - block) & (part + low < begin)
+            update = mm(pans[before, :, other], pans[before, :, place], ((0,), (0,)))
+            work[other, place] = jnp.where(gone, 0.0, work[other, place]) - update
+
         rows = [
-            t_ref[pl.ds(pl.multiple_of(begin + p * PANEL, PANEL), PANEL), own]
-            for p in range(block // PANEL)
+            work[pl.ds(pl.multiple_of(begin + p * PANEL, PANEL), PANEL), own]
+            for p in range(turns)
         ]
-        upper, lower = factor_block(rows, block)
-        pan[...] = mm(lower, t_ref[own, :], ((1,), (0,)))
-        pan[:, own] = lower
-
-        def trail(i, inner):
-            other = pl.ds(pl.multiple_of(i * block, block), block)
-            t_ref[other, own] = jnp.zeros((block, block), jnp.float32)
-            t_ref[other, :] = t_ref[other, :] - mm(pan[:, other], pan[...], ((0,), (0,)))
-            return inner
-
-        lax.fori_loop(k + 1, blocks, trail, 0)
+        upper, lower = factor_block(rows, block, beside)
+        pans[now, :, :width] = mm(lower, work[own, :], ((1,), (0,)))
+        pans[now, :, own] = lower
+        pan = pans[now, :, :width]
         after = column >= begin + block
-        r_ref[own, :] = jnp.where(after, pan[...], 0.0)
+        following = pl.ds(pl.multiple_of(begin + block, block), block)
+        gone = (column >= begin) & (column < begin + block)
+        update = mm(pans[now, :, following], pan, ((0,), (0,)))
+        work[following, :] = jnp.where(gone, 0.0, work[following, :]) - update
+        r_ref[own, :] = jnp.where(after, pan, 0.0)
         r_ref[own, own] = upper
-        t_ref[own, :] = jnp.where(after, 0.0, pan[...])
+        t_ref[own, :] = jnp.where(after, 0.0, pan)
         return carry
 
     lax.fori_loop(0, blocks, step, 0)
@@ -152,12 +172,20 @@
         out_shape=(whole, whole),
         in_specs=[pl.BlockSpec(memory_space=pltpu.VMEM)],
         out_specs=(pl.BlockSpec(memory_space=pltpu.VMEM),) * 2,
-        scratch_shapes=[pltpu.VMEM((LANES, width), jnp.float32)],
-        compiler_params=pltpu.CompilerParams(vmem_limit_bytes=40 * 1024 * 1024),
+        scratch_shapes=[
+            pltpu.VMEM((width + LANES, width), jnp.float32),
+            pltpu.VMEM((2, LANES, width + LANES), jnp.float32),
+        ],
+        compiler_params=pltpu.CompilerParams(vmem_limit_bytes=32 * 1024 * 1024),
         cost_estimate=pl.CostEstimate(
             flops=100 * width**3, bytes_accessed=12 * width * width, transcendentals=0
         ),
     )(folded)
+
+
+def basis_kernel(a_ref, inverse_ref, x_ref, basis):
+    basis[...] = mm(a_ref[...], inverse_ref[...], ((1,), (1,)))
+    gram_kernel(basis, x_ref)
 
 
 def gram_kernel(basis_ref, x_ref):
@@ -186,22 +214,50 @@
             x_ref[i * tiles : (i + 1) * tiles, j] = value.reshape(tiles, 8, LANES)
 
 
-def folded_gram(basis, devices):
+def folded_gram(basis, devices, inverse=None):
     width = basis.shape[1]
     lanes = width // LANES
     count = width // 16 + 1
     while count * lanes % (2 * devices):
         count += 1
+    operands = (basis,) if inverse is None else (basis, inverse)
     return pl.pallas_call(
-        gram_kernel,
+        gram_kernel if inverse is None else basis_kernel,
         out_shape=jax.ShapeDtypeStruct((count, lanes, 8, LANES), jnp.float32),
-        in_specs=[pl.BlockSpec(memory_space=pltpu.VMEM)],
+        in_specs=[pl.BlockSpec(memory_space=pltpu.VMEM)] * len(operands),
         out_specs=pl.BlockSpec(memory_space=pltpu.VMEM),
+        scratch_shapes=[] if inverse is None else [pltpu.VMEM(basis.shape, jnp.float32)],
         compiler_params=pltpu.CompilerParams(vmem_limit_bytes=24 * 1024 * 1024),
         cost_estimate=pl.CostEstimate(
             flops=12 * basis.shape[0] * width**2, bytes_accessed=8 * basis.size, transcendentals=0
         ),
-    )(basis)
+    )(*operands)
+
+
+def cross_kernel(a_ref, b_ref, c_ref):
+    for i in range(a_ref.shape[1] // LANES):
+        own = slice(i * LANES, (i + 1) * LANES)
+        c_ref[own, :] = mm(a_ref[:, own], b_ref[...], ((0,), (0,)))
+
+
+def tail_kernel(second_ref, rows_ref, upper_ref, inverse_ref, cross_ref, factor_ref, out_ref):
+    factor_ref[...] = mm(second_ref[...], upper_ref[...], ((1,), (0,)))
+    rows = mm(rows_ref[...], inverse_ref[...], ((1,), (0,)))
+    out_ref[...] = mm(rows, cross_ref[...], ((1,), (0,)))
+
+
+def in_vmem(kernel, out_shape, flops, *operands):
+    outs = len(out_shape)
+    return pl.pallas_call(
+        kernel,
+        out_shape=out_shape,
+        in_specs=[pl.BlockSpec(memory_space=pltpu.VMEM)] * len(operands),
+        out_specs=(pl.BlockSpec(memory_space=pltpu.VMEM),) * outs,
+        compiler_params=pltpu.CompilerParams(vmem_limit_bytes=24 * 1024 * 1024),
+        cost_estimate=pl.CostEstimate(
+            flops=flops, bytes_accessed=4 * sum(x.size for x in operands), transcendentals=0
+        ),
+    )(*operands)
 
 
 def sum_kernel(orders, x_ref, out_ref, *scratch):
@@ -302,9 +358,9 @@
     )(tiles)
 
 
-def sum_gram(basis):
+def sum_gram(basis, inverse=None):
     devices = lax.axis_size("row")
-    folded = folded_gram(basis, devices)
+    folded = folded_gram(basis, devices, inverse)
     return sum_tiles(folded.reshape(-1, 8, LANES), devices).reshape(folded.shape)
 
 
@@ -312,20 +368,32 @@
     width = matrix_a.shape[1]
     out_rows = width // lax.axis_size("row")
     start = lax.axis_index("row") * out_rows
+    whole = jax.ShapeDtypeStruct((width, width), jnp.float32)
+    share = jax.ShapeDtypeStruct((out_rows, width), jnp.float32)
     gram1 = sum_gram(matrix_a)
-    cross = mm(matrix_a, matrix_b, ((0,), (0,)))
+    (cross,) = in_vmem(
+        cross_kernel, (whole,), 12 * matrix_a.shape[0] * width**2, matrix_a, matrix_b
+    )
     gram1, cross = lax.optimization_barrier((gram1, cross))
-    cross = lax.psum(cross, "row")
+    cross = lax.psum_scatter(cross, "row", scatter_dimension=0, tiled=True)
     upper1, inverse1 = factor_pair(gram1, width, True)
-    basis1 = mm(matrix_a, inverse1, ((1,), (1,)))
-    gram2 = sum_gram(basis1)
+    gram2 = sum_gram(matrix_a, inverse1)
+    gram2, cross = lax.optimization_barrier((gram2, cross))
+    cross = lax.all_gather(cross, "row", axis=0, tiled=True)
     upper2, inverse2 = factor_pair(gram2, width, False)
     first_rows = lax.dynamic_slice_in_dim(upper1, start, out_rows, 0)
     second_rows = lax.dynamic_slice_in_dim(upper2, start, out_rows, 0)
     inverse_rows = lax.dynamic_slice_in_dim(inverse2, start, out_rows, 0)
-    factor_rows = mm(second_rows, upper1, ((1,), (0,)))
-    inverse_rows = mm(inverse_rows, inverse1, ((1,), (0,)))
-    projection = mm(inverse_rows, cross, ((1,), (0,)))
+    factor_rows, projection = in_vmem(
+        tail_kernel,
+        (share, share),
+        36 * out_rows * width**2,
+        second_rows,
+        inverse_rows,
+        upper1,
+        inverse1,
+        cross,
+    )
     return (first_rows, factor_rows, projection)
 
 

time: 284 us -> 241 us (0.85)
  matrix products: 24.5 us -> 0 us
  Pallas kernels: 236 us -> 216 us
    dot_general x5 -> x0, matrix products: 24.5 us -> none  [mm(): lax.dot_general(x, y, (dims, ((), ())), precision=HIGHEST, preferred_elem...]
    pallas_call x2, Pallas kernels: 122 us -> 104 us  [factor_pair(): pl.pallas_call(functools.partial(factor_kernel, LANES, shifted), out_shap...]
    pallas_call x2, Pallas kernels: 109 us -> 92.6 us  [sum_tiles(): pl.pallas_call(functools.partial(sum_kernel, orders), out_shape=jax.Shape...]
    pallas_call x2 -> x4, Pallas kernels: 4.73 us -> 19.9 us  [the longest x2 11.3 us: in_vmem(): pl.pallas_call(kernel, out_shape=out_shape, in_specs=[pl.BlockSpec(memory...]
    unnamed x20 -> x18, local copies, waits for them, and re-layouts: 8.13 us -> 9.67 us
  transfers between devices with their start and end apart: 1 -> 2, of which waited for: 0 -> 0; matrix products, arithmetic and copies ran while one was open for 5% -> 0% of each run, Pallas kernels for 66% -> 66%
where the time goes in v4:
time: 241 us
  Pallas kernels  216 us (90%)
  between operations  14.2 us (6%)
  local copies, waits for them, and re-layouts  10.5 us (4%)
    pallas_call x2, Pallas kernels, factor_pair(): pl.pallas_call(functools.partial(factor_kernel, LANES, shifted), out_shap...  104 us
    pallas_call x2, Pallas kernels, sum_tiles(): pl.pallas_call(functools.partial(sum_kernel, orders), out_shape=jax.Shape...  92.6 us
    pallas_call x2, Pallas kernels, in_vmem(): pl.pallas_call(kernel, out_shape=out_shape, in_specs=[pl.BlockSpec(memory...  11.3 us
    unnamed x18, local copies, waits for them, and re-layouts  9.67 us
    pallas_call x2, Pallas kernels, folded_gram(): pl.pallas_call(gram_kernel if inverse is None else basis_kernel, out_shap...  8.63 us
  transfers between devices with their start and end apart: 2, of which 0 were waited for; matrix products, arithmetic and copies ran while one was open for 0% of the time, Pallas kernels for 66%

profile of v4, /device:TPU:0, one launch (start us, length us, event | category | flops | bytes accessed | tf_op | source)
XLA Modules:
  0.0 241.2 jit_solution(13346608604020483194)
XLA Ops:
  7.2 0.0 reduce-scatter.2.cloned.1.call-start
  7.2 0.0 copy-start.7
  7.2 1.1 copy-done.7
  8.3 2.4 shard_map.49
  10.7 0.0 copy-start.6
  10.7 0.0 copy-start.8
  10.7 44.5 %shard_map.50 = f32[544,8,128]{2,1,0:T(8,128)S(1)} custom-call(f32[544,8,128]{2,1,0:T(8,128)S(1)} %bitcast.6), custom_call_target="tpu_custom_call" | custom-call | flops 8589934592 | bytes 4456448 | tf_op jit(solution)/shard_map/pallas_call | solution.py:346
  55.3 0.0 copy-done.6
  55.3 0.0 copy-done.8
  55.3 3.6 %shard_map.51 = f32[1024,1024]{1,0:T(8,128)S(1)} custom-call(f32[192,1024]{1,0:T(8,128)S(1)} %copy-done.8, f32[192,1024]{1,0:T(8,128)S(1)} %copy-done.6), custom_call_target="tpu_custom_call" | custom-call | flops 2415919104 | bytes 1572864 | tf_op jit(solution)/shard_map/pallas_call | solution.py:251
  58.9 0.0 copy-start.5
  58.9 2.0 copy-done.5
  60.9 0.0 reduce-scatter.2.cloned.1.call-update
  60.9 0.0 all-gather.2.cloned.1.call-start
  60.9 51.9 %shard_map.52 = (f32[1024,1024]{1,0:T(8,128)S(1)}, f32[1024,1024]{1,0:T(8,128)S(1)}) custom-call(f32[68,8,8,128]{3,2,1,0:T(8,128)S(1)} %bitcast.4), custom_call_target="tpu_custom_call" | custom-call | flops 107374182400 | bytes 12582912 | tf_op jit(solution)/shard_map/pallas_call | solution.py:170
  112.9 0.0 copy-start
  112.9 0.0 copy-start.2
  112.9 0.8 constant_dynamic-slice_fusion.2
  113.7 6.3 %shard_map.53 = f32[68,8,8,128]{3,2,1,0:T(8,128)S(1)} custom-call(f32[192,1024]{1,0:T(8,128)S(1)} %copy-done.8, f32[1024,1024]{1,0:T(8,128)S(1)} %get-tuple-element.15.inverse_ref), custom_call_target="tpu_custom_call" | custom-call | flops 2415919104 | bytes 1572864 | tf_op jit(solution)/shard_map/pallas_call | solution.py:224
  120.0 0.0 copy-done
  120.0 0.0 copy-done.2
  120.0 48.0 %shard_map.54 = f32[544,8,128]{2,1,0:T(8,128)S(1)} custom-call(f32[544,8,128]{2,1,0:T(8,128)S(1)} %bitcast.7), custom_call_target="tpu_custom_call" | custom-call | flops 8589934592 | bytes 4456448 | tf_op jit(solution)/shard_map/pallas_call | solution.py:346
  168.0 0.0 reduce-scatter.2.cloned.1.call-done
  168.1 0.0 all-gather.2.cloned.1.call-update
  168.1 51.9 %shard_map.55 = (f32[1024,1024]{1,0:T(8,128)S(1)}, f32[1024,1024]{1,0:T(8,128)S(1)}) custom-call(f32[68,8,8,128]{3,2,1,0:T(8,128)S(1)} %bitcast.5), custom_call_target="tpu_custom_call" | custom-call | flops 107374182400 | bytes 12582912 | tf_op jit(solution)/shard_map/pallas_call | solution.py:170
  220.0 0.0 all-gather.2.cloned.1.call-done.cross_ref
  220.0 0.0 copy-start.1
  220.0 2.2 copy-done.1
  222.2 0.0 copy-start.3
  222.2 2.2 copy-done.3
  224.4 0.0 copy-start.4
  224.4 2.2 copy-done.4
  226.6 7.7 %shard_map.56 = (f32[64,1024]{1,0:T(8,128)}, f32[64,1024]{1,0:T(8,128)}) custom-call(f32[64,1024]{1,0:T(8,128)S(1)} %get-tuple-element.24.second_ref, f32[64,1024]{1,0:T(8,128)S(1)} %get-tuple-element.23.rows_ref, f32[1024,1024]{1,0:T(8,128)S(1)} %copy-done.1, f32[1024,1024]{1,0:T(8,128)S(1)} %copy-done.3, f32[1024,1024]{1,0:T(8,128)S(1)} %copy-done.4), custom_call_target="tpu_custom_call" | custom-call | flops 2415919104 | bytes 13107200 | tf_op jit(solution)/shard_map/pallas_call | solution.py:251
  (1 shorter events, 0.0 us)
Async XLA Ops:
  7.2 160.9 %reduce-scatter.2.cloned.1.call-start = ((), (), s32[]{:S(2)}) async-start(), calls=%async_computation.1 | async-start | bytes 4456448 | tf_op jit(solution)/shard_map/reduce_scatter | solution.py:378
  7.2 1.1 copy-start.7
  10.7 44.6 %copy-start.6 = (f32[192,1024]{1,0:T(8,128)S(1)}, f32[192,1024]{1,0:T(8,128)}, u32[]{:S(2)}) copy-start(f32[192,1024]{1,0:T(8,128)} %b_ref.1) | copy-start | bytes 2359300
  10.7 44.6 %copy-start.8 = (f32[192,1024]{1,0:T(8,128)S(1)}, f32[192,1024]{1,0:T(8,128)}, u32[]{:S(2)}) copy-start(f32[192,1024]{1,0:T(8,128)} %a_ref.3) | copy-start | bytes 2359300
  58.9 2.0 copy-start.5
  60.9 159.2 %all-gather.2.cloned.1.call-start = ((), (), s32[]{:S(2)}) async-start(), calls=%async_computation.2 | async-start | bytes 4456448 | tf_op jit(solution)/shard_map/all_gather | solution.py:382
  112.9 7.1 %copy-start = (f32[1024,1024]{1,0:T(8,128)}, f32[1024,1024]{1,0:T(8,128)S(1)}, u32[]{:S(2)}) copy-start(f32[1024,1024]{1,0:T(8,128)S(1)} %get-tuple-element.14.upper_ref) | copy-start | bytes 12582916
  112.9 7.1 %copy-start.2 = (f32[1024,1024]{1,0:T(8,128)}, f32[1024,1024]{1,0:T(8,128)S(1)}, u32[]{:S(2)}) copy-start(f32[1024,1024]{1,0:T(8,128)S(1)} %get-tuple-element.15.inverse_ref) | copy-start | bytes 12582916
  220.0 2.2 copy-start.1
  222.2 2.2 copy-start.3
  224.4 2.2 copy-start.4
Sparse Core Ops, SparseCore 0:
  61.0 75.3 reduce-scatter.1
  168.2 49.7 all-gather.1
